TPU v7x, 32 devices: a whole 2x2x4 slice. The times are simulated.
32 devices in a mesh: section: 2 (over core), dp: 16 (over z, y, x).
Axes of the slice: x: 2, y: 2, z: 4, core: 2. Of those that a mesh axis runs over, the one named last changes fastest.
Arguments:
- hidden_in: bfloat16 [16384, 768], P('dp')
- segment_ids: int32 [32, 512], P('dp'), may hold values from 0 to 8, as said below
- cls_positions: int32 [32, 8], P('dp'), may hold values from 0 to 361, as said below
- valid_counts: int32 [32], P('dp'), may hold values from 224 to 512, as said below
- proj_in: bfloat16 [2, 768, 2304], P('section'), may hold values from -0.21875 to 0.21875
- proj_bias: float32 [2, 2, 768], P('section'), may hold values from -1.2 to 1.2
- proj_out: bfloat16 [2, 768, 768], P('section'), may hold values from -1.25 to 1.25
- out_shift: float32 [2, 768], P('section'), may hold values from -1.2 to 1.2
- norm_gains: float32 [2, 2, 768], P('section'), may hold values from 0.25 to 1.75
- norm_shifts: float32 [2, 2, 768], P('section'), may hold values from -1.2 to 1.2
- widen: bfloat16 [2, 768, 3072], P('section'), may hold values from -0.21875 to 0.21875
- widen_bias: float32 [2, 3072], P('section'), may hold values from -1.2 to 1.2
- narrow: bfloat16 [2, 3072, 768], P('section'), may hold values from -0.109375 to 0.109375
- narrow_bias: float32 [2, 768], P('section'), may hold values from -1.2 to 1.2
- cotangent: bfloat16 [16384, 768], P('dp'), may hold values from -6 to 6
Outputs:
- section_cls: float32 [2, 32, 8, 768], P('section', 'dp')
- section_input_grads: float32 [2, 16384, 768], P('section', 'dp')
- proj_in_grad: float32 [2, 768, 2304], P('section')
- proj_bias_grad: float32 [2, 2, 768], P('section')
- proj_out_grad: float32 [2, 768, 768], P('section')
- out_shift_grad: float32 [2, 768], P('section')
- norm_gain_grad: float32 [2, 2, 768], P('section')
- norm_shift_grad: float32 [2, 2, 768], P('section')
- widen_grad: float32 [2, 768, 3072], P('section')
- widen_bias_grad: float32 [2, 3072], P('section')
- narrow_grad: float32 [2, 3072, 768], P('section')
- narrow_bias_grad: float32 [2, 768], P('section')
- stream_rms: float32 [2, 3], P('section')
Inputs may be any that keep to these rules, and one draw needn't show every extreme that they name: `segment_ids`: each row holds 8 segments in order, numbered 0 up, a query then a passage in turn, followed by padding numbered 8 up to the row's end. `cls_positions`: the first position of each segment of the row, rising. `valid_counts`: the sum of the row's segment lengths; the positions from it on are padding. Some row has no padding.
All inputs are finite; a program needn't handle non-finite values.
Results may differ from a plain program's by a relative error of at most 0.019.
The roundings to bfloat16 on the way count: a program that leaves them out, or rounds other values in their place, can miss the bound.
Values may be sent and summed in bfloat16 or wider, within the bound.
A program may use at most 320 MiB of HBM per device.

v0:
```python
from functools import partial

import jax
import jax.numpy as jnp
from jax import lax
from jax.sharding import PartitionSpec as P

HEADS = 12
HEAD_DIM = 64


EPSILON = 1e-12
MASKED = -1e30


def shifted(block, axis, distance):
    devices = range(lax.axis_size(axis))
    route = [(i - distance, i) for i in devices if i - distance in devices]
    return lax.ppermute(block, axis, route)


def matmul(left, right):
    return jnp.dot(left, right, preferred_element_type=jnp.float32)


def matmul_left_t(left, right):
    return lax.dot_general(
        left, right, (((0,), (0,)), ((), ())), preferred_element_type=jnp.float32
    )


def matmul_right_t(left, right):
    return lax.dot_general(
        left, right, (((1,), (1,)), ((), ())), preferred_element_type=jnp.float32
    )


def to_half(array):
    return array.astype(jnp.bfloat16)


def by_section(section_no, options):
    chosen = options[0]
    chosen = jax.tree.map(
        lambda kept, other: jnp.where(section_no == 1, other, kept), chosen, options[1]
    )
    return chosen


def normalize(signal):
    centred = signal - jnp.mean(signal, -1, keepdims=True)
    factor = lax.rsqrt(jnp.mean(centred * centred, -1, keepdims=True) + EPSILON)
    return (centred * factor, factor)


def normalize_back(upstream, normed, factor):
    return factor * (
        upstream
        - jnp.mean(upstream, -1, keepdims=True)
        - normed * jnp.mean(upstream * normed, -1, keepdims=True)
    )


def attention_scores(qkv_parts, segments):
    scores = jnp.einsum(
        "qhd,khd->hqk", qkv_parts[:, 0], qkv_parts[:, 1], preferred_element_type=jnp.float32
    ) * HEAD_DIM ** (-0.5)
    same_doc = segments[:, None] == segments[None, :]
    return jnp.where(same_doc[None], scores, MASKED)


def forward_row(layer_in, segments, params):
    (
        proj_in,
        proj_bias,
        proj_out,
        out_shift,
        norm_gains,
        norm_shifts,
        widen,
        widen_bias,
        narrow,
        narrow_bias,
    ) = params
    length = layer_in.shape[0]
    model_width = proj_out.shape[0]
    filler = jnp.zeros_like(proj_bias[0])
    qkv_all = to_half(
        matmul(layer_in, proj_in) + jnp.concatenate([proj_bias[0], filler, proj_bias[1]])
    )
    qkv_parts = qkv_all.reshape(length, 3, HEADS, HEAD_DIM)
    scores = attention_scores(qkv_parts, segments)
    highest = jnp.max(scores, -1, keepdims=True)
    raised = jnp.exp(scores - highest)
    totals = jnp.sum(raised, -1, keepdims=True)
    weights = to_half(raised / totals)
    log_total = highest + jnp.log(totals)
    mixed_heads = to_half(
        jnp.einsum(
            "hqk,khd->qhd", weights, qkv_parts[:, 2], preferred_element_type=jnp.float32
        ).reshape(length, model_width)
    )
    branch = matmul(mixed_heads, proj_out) + out_shift
    normed_first, factor_first = normalize(layer_in.astype(jnp.float32) + branch)
    first_out = normed_first * norm_gains[0] + norm_shifts[0]
    hidden = matmul(to_half(first_out), widen) + widen_bias
    activated = to_half(jax.nn.gelu(hidden, approximate=False))
    feed_out = matmul(activated, narrow) + narrow_bias
    stream = first_out + feed_out
    normed_second, factor_second = normalize(stream)
    result = normed_second * norm_gains[1] + norm_shifts[1]
    saved = (
        qkv_all,
        log_total,
        mixed_heads,
        normed_first,
        factor_first,
        hidden,
        normed_second,
        factor_second,
    )
    return (result, saved, (stream, branch, feed_out))


def feed_back(upstream, saved, params):
    (
        proj_in,
        proj_bias,
        proj_out,
        out_shift,
        norm_gains,
        norm_shifts,
        widen,
        widen_bias,
        narrow,
        narrow_bias,
    ) = params
    (
        qkv_all,
        log_total,
        mixed_heads,
        normed_first,
        factor_first,
        hidden,
        normed_second,
        factor_second,
    ) = saved
    gain_second = jnp.sum(upstream * normed_second, 0)
    shift_second = jnp.sum(upstream, 0)
    d_stream = normalize_back(upstream * norm_gains[1], normed_second, factor_second)
    d_feed = to_half(d_stream)
    activated = to_half(jax.nn.gelu(hidden, approximate=False))
    grad_narrow = matmul_left_t(activated, d_feed)
    grad_narrow_bias = jnp.sum(d_feed.astype(jnp.float32), 0)
    gelu_out, gelu_back = jax.vjp(partial(jax.nn.gelu, approximate=False), hidden)
    d_hidden = to_half(gelu_back(matmul_right_t(d_feed, narrow))[0])
    first_out = normed_first * norm_gains[0] + norm_shifts[0]
    grad_widen = matmul_left_t(to_half(first_out), d_hidden)
    grad_widen_bias = jnp.sum(d_hidden.astype(jnp.float32), 0)
    d_first = d_stream + matmul_right_t(d_hidden, widen)
    return (
        d_first,
        (gain_second, shift_second, grad_widen, grad_widen_bias, grad_narrow, grad_narrow_bias),
    )


def attention_back(d_first, layer_in, segments, saved, params):
    (
        proj_in,
        proj_bias,
        proj_out,
        out_shift,
        norm_gains,
        norm_shifts,
        widen,
        widen_bias,
        narrow,
        narrow_bias,
    ) = params
    (
        qkv_all,
        log_total,
        mixed_heads,
        normed_first,
        factor_first,
        hidden,
        normed_second,
        factor_second,
    ) = saved
    length = layer_in.shape[0]
    model_width = proj_out.shape[0]
    gain_first = jnp.sum(d_first * normed_first, 0)
    shift_first = jnp.sum(d_first, 0)
    d_resid = normalize_back(d_first * norm_gains[0], normed_first, factor_first)
    d_branch = to_half(d_resid)
    grad_out = matmul_left_t(mixed_heads, d_branch)
    grad_out_shift = jnp.sum(d_branch.astype(jnp.float32), 0)
    d_mixed = to_half(matmul_right_t(d_branch, proj_out)).reshape(length, HEADS, HEAD_DIM)
    qkv_parts = qkv_all.reshape(length, 3, HEADS, HEAD_DIM)
    probs = jnp.exp(attention_scores(qkv_parts, segments) - log_total)
    d_probs = jnp.einsum(
        "qhd,khd->hqk", d_mixed, qkv_parts[:, 2], preferred_element_type=jnp.float32
    )
    d_scores = to_half(probs * (d_probs - jnp.sum(probs * d_probs, -1, keepdims=True)))
    scale_factor = HEAD_DIM ** (-0.5)
    d_query = (
        jnp.einsum("hqk,khd->qhd", d_scores, qkv_parts[:, 1], preferred_element_type=jnp.float32)
        * scale_factor
    )
    d_key = (
        jnp.einsum("hqk,qhd->khd", d_scores, qkv_parts[:, 0], preferred_element_type=jnp.float32)
        * scale_factor
    )
    d_value = jnp.einsum(
        "hqk,qhd->khd", to_half(probs), d_mixed, preferred_element_type=jnp.float32
    )
    d_qkv = to_half(jnp.stack([d_query, d_key, d_value], 1).reshape(length, 3 * model_width))
    grad_in = matmul_left_t(layer_in, d_qkv)
    column_sums = jnp.sum(d_qkv.astype(jnp.float32), 0).reshape(3, model_width)
    grad_bias = jnp.stack([column_sums[0], column_sums[2]])
    d_layer_in = d_resid + matmul_right_t(d_qkv, proj_in)
    return (d_layer_in, (grad_in, grad_bias, grad_out, grad_out_shift, gain_first, shift_first))


def local(
    hidden_in,
    segment_ids,
    cls_positions,
    valid_counts,
    proj_in,
    proj_bias,
    proj_out,
    out_shift,
    norm_gains,
    norm_shifts,
    widen,
    widen_bias,
    narrow,
    narrow_bias,
    cotangent,
):
    params = tuple(
        (
            array[0]
            for array in (
                proj_in,
                proj_bias,
                proj_out,
                out_shift,
                norm_gains,
                norm_shifts,
                widen,
                widen_bias,
                narrow,
                narrow_bias,
            )
        )
    )
    section_count = lax.axis_size("section")
    section_no = lax.axis_index("section")
    row_count, length = segment_ids.shape
    model_width = hidden_in.shape[1]
    inputs = hidden_in.reshape(row_count, length, model_width)
    upstreams = cotangent.reshape(row_count, length, model_width)
    tick_count = row_count + section_count - 1
    positions = jnp.arange(length, dtype=jnp.int32)
    received = jnp.zeros((length, model_width), jnp.bfloat16)
    square_sums = jnp.zeros((3,), jnp.float32)
    saved_list = []
    output_list = []
    for tick_no in range(tick_count):
        micro_no = tick_no - section_no
        is_live = ((micro_no >= 0) & (micro_no < row_count)).astype(jnp.float32)
        row_slot = jnp.clip(micro_no, 0, row_count - 1)
        layer_in = jnp.where(section_no == 0, inputs[min(tick_no, row_count - 1)], received)
        segments = lax.dynamic_index_in_dim(segment_ids, row_slot, 0, keepdims=False)
        result, saved, stats = forward_row(layer_in, segments, params)
        row_limit = lax.dynamic_index_in_dim(valid_counts, row_slot, 0, keepdims=False)
        row_valid = (positions < row_limit).astype(jnp.float32)[:, None]
        square_sums = square_sums + is_live * jnp.stack(
            [jnp.sum(row_valid * summand * summand) for summand in stats]
        )
        saved_list.append((layer_in, saved))
        output_list.append(result)
        if tick_no + 1 < tick_count:
            received = shifted(to_half(result), "section", 1)
    token_count = jnp.sum(valid_counts.astype(jnp.float32))
    stat_total = lax.psum((square_sums, token_count), "dp")
    back_received = jnp.zeros((length, model_width), jnp.bfloat16)
    grads = [jnp.zeros(array.shape, jnp.float32) for array in params]
    input_grads = []
    for tick_no in range(tick_count):
        micro_no = tick_no - (section_count - 1 - section_no)
        is_live = ((micro_no >= 0) & (micro_no < row_count)).astype(jnp.float32)
        row_slot = jnp.clip(micro_no, 0, row_count - 1)
        candidates = [
            saved_list[min(max(tick_no - (section_count - 1) + 2 * option_no, 0), tick_count - 1)]
            for option_no in range(section_count)
        ]
        layer_in, saved = by_section(section_no, candidates)
        segments = lax.dynamic_index_in_dim(segment_ids, row_slot, 0, keepdims=False)
        own_grad = lax.dynamic_index_in_dim(upstreams, row_slot, 0, keepdims=False).astype(
            jnp.float32
        )
        upstream = jnp.where(
            section_no == section_count - 1, own_grad, back_received.astype(jnp.float32)
        )
        d_first, feed_grads = feed_back(upstream, saved, params)
        gain_second, shift_second, grad_widen, grad_widen_bias, grad_narrow, grad_narrow_bias = (
            feed_grads
        )
        grads[6] = grads[6] + is_live * grad_widen
        grads[7] = grads[7] + is_live * grad_widen_bias
        grads[8] = grads[8] + is_live * grad_narrow
        grads[9] = grads[9] + is_live * grad_narrow_bias
        grads[4] = grads[4].at[1].add(is_live * gain_second)
        grads[5] = grads[5].at[1].add(is_live * shift_second)
        d_layer_in, attn_grads = attention_back(d_first, layer_in, segments, saved, params)
        grad_in, grad_bias, grad_out, grad_out_shift, gain_first, shift_first = attn_grads
        grads[0] = grads[0] + is_live * grad_in
        grads[1] = grads[1] + is_live * grad_bias
        grads[2] = grads[2] + is_live * grad_out
        grads[3] = grads[3] + is_live * grad_out_shift
        grads[4] = grads[4].at[0].add(is_live * gain_first)
        grads[5] = grads[5].at[0].add(is_live * shift_first)
        input_grads.append(d_layer_in)
        if tick_no + 1 < tick_count:
            back_received = shifted(to_half(d_layer_in), "section", -1)
    big_shards = (
        lax.psum_scatter(grads[0], "dp", scatter_dimension=0, tiled=True),
        lax.psum_scatter(grads[2], "dp", scatter_dimension=0, tiled=True),
        lax.psum_scatter(grads[6], "dp", scatter_dimension=0, tiled=True),
        lax.psum_scatter(grads[8], "dp", scatter_dimension=0, tiled=True),
    )
    big_totals = (
        lax.all_gather(big_shards[0].astype(jnp.bfloat16), "dp", axis=0, tiled=True).astype(
            jnp.float32
        ),
        lax.all_gather(big_shards[1].astype(jnp.bfloat16), "dp", axis=0, tiled=True).astype(
            jnp.float32
        ),
        lax.all_gather(big_shards[2].astype(jnp.bfloat16), "dp", axis=0, tiled=True).astype(
            jnp.float32
        ),
        lax.all_gather(big_shards[3].astype(jnp.bfloat16), "dp", axis=0, tiled=True).astype(
            jnp.float32
        ),
    )
    small_totals = lax.psum((grads[1], grads[3], grads[4], grads[5], grads[7], grads[9]), "dp")
    square_total = stat_total[0]
    count_total = stat_total[1]
    stream_rms = jnp.sqrt(square_total / (count_total * model_width))
    own_outputs = by_section(
        section_no,
        [
            jnp.stack(output_list[option_no : option_no + row_count])
            for option_no in range(section_count)
        ],
    )
    selector = (positions[None, None, :] == cls_positions[:, :, None]).astype(jnp.float32)
    section_cls = jnp.einsum("rnl,rld->rnd", selector, own_outputs, precision=lax.Precision.HIGHEST)
    own_grads = by_section(
        section_no,
        [
            jnp.stack(
                input_grads[
                    section_count - 1 - option_no : section_count - 1 - option_no + row_count
                ]
            )
            for option_no in range(section_count)
        ],
    )
    return (
        section_cls[None],
        own_grads.reshape(1, row_count * length, model_width),
        big_totals[0][None],
        small_totals[0][None],
        big_totals[1][None],
        small_totals[1][None],
        small_totals[2][None],
        small_totals[3][None],
        big_totals[2][None],
        small_totals[4][None],
        big_totals[3][None],
        small_totals[5][None],
        stream_rms[None],
    )


def solution(mesh):
    placed = (
        P("dp", None),
        P("dp", None),
        P("dp", None),
        P("dp"),
        P("section", None, None),
        P("section", None, None),
        P("section", None, None),
        P("section", None),
        P("section", None, None),
        P("section", None, None),
        P("section", None, None),
        P("section", None),
        P("section", None, None),
        P("section", None),
        P("dp", None),
    )
    return jax.shard_map(
        local,
        mesh=mesh,
        in_specs=placed,
        out_specs=(
            P("section", "dp", None, None),
            P("section", "dp", None),
            P("section", None, None),
            P("section", None, None),
            P("section", None, None),
            P("section", None),
            P("section", None, None),
            P("section", None, None),
            P("section", None, None),
            P("section", None),
            P("section", None, None),
            P("section", None),
            P("section", None),
        ),
        check_vma=False,
    )
```

profile of v0, /device:TPU:0, one launch (start us, length us, event | category | flops | bytes accessed | tf_op | source)
XLA Modules:
  0.0 1395.9 jit_solution(7476712655474664674)
XLA Ops:
  47.6 22.0 %fusion.468 = (f32[512]{0:T(512)S(1)}, f32[512,768]{1,0:T(8,128)S(1)}, f32[512,768]{1,0:T(8,128)}) fusion(f32[768]{0:T(1024)S(1)} %copy-done.120, f32[768]{0:T(1024)S(1)} %get-tuple-element.189, f32[768]{0:T(1024)S(1)} %get-tuple-element.329, f32[512]{0:T(512)S(1)} %copy-done.145, f32[512,768]{1,0:T(8,128)S(1)} %copy-done.61, f32[512]{0:T(512)S(1)} %copy-done.132, ...), kind=kOutput, calls=%fused_computation.730 | convolution fusion | flops 2522480128 | bytes 15756288 | tf_op jit(solution)/shard_map/dot_general | solution.py:23
  115.7 17.2 %fusion.466 = (f32[512]{0:T(512)S(1)}, f32[512,768]{1,0:T(8,128)S(1)}, f32[512,768]{1,0:T(8,128)}) fusion(f32[768]{0:T(1024)S(1)} %copy-done.121, f32[768]{0:T(1024)S(1)} %get-tuple-element.189, f32[768]{0:T(1024)S(1)} %get-tuple-element.329, f32[512]{0:T(512)S(1)} %add_rsqrt_fusion.3, f32[512,768]{1,0:T(8,128)S(1)} %get-tuple-element.246, ...), kind=kOutput, calls=%fused_computation.728 | convolution fusion | flops 2522480128 | bytes 15756288 | tf_op jit(solution)/shard_map/dot_general | solution.py:23
  176.1 33.5 %fusion.19 = (f32[512,3072]{1,0:T(8,128)}, f32[512,3072]{1,0:T(8,128)}, f32[512,3072]{1,0:T(8,128)S(1)}, f32[512,3072]{1,0:T(8,128)S(1)}, f32[512,3072]{1,0:T(8,128)}) fusion(f32[512,3072]{1,0:T(8,128)} %copy-done.161, f32[3072]{0:T(1024)S(1)} %bitcast.434, pred[]{:T(512)S(6)} %eq.169, f32[512,3072]{1,0:T(8,128)} %copy-done.160, ...), kind=kOutput, calls=%fused_computation.46 | convolution fusion | flops 2620784640 | bytes 50354176 | tf_op jit(solution)/shard_map/dot_general | solution.py:23
  209.7 12.0 convert_reduce_fusion.2
  221.8 8.2 multiply_reduce_fusion.7
  230.1 18.4 %convert_reduce_fusion.11 = (f32[768]{0:T(1024)}, f32[512,768]{1,0:T(8,128)S(1)}, f32[512]{0:T(512)S(1)}, f32[512,768]{1,0:T(8,128)}, f32[512,768]{1,0:T(8,128)}) fusion(f32[512,768]{1,0:T(8,128)S(1)} %get-tuple-element.235, f32[512]{0:T(512)S(1)} %broadcast_multiply_fusion.20, f32[512]{0:T(512)S(1)} %broadcast_multiply_fusion.21, ...), kind=kOutput, calls=%fused_computation.344 | convolution fusion | flops 2525625088 | bytes 20484096 | tf_op jit(solution)/shard_map/dot_general | solution.py:23
  264.4 8.0 multiply_reduce_fusion.2
  272.3 7.4 multiply_convert_fusion.2
  298.6 7.7 fusion.321
  321.2 8.2 fusion.322
  334.6 9.2 convert_reduce_fusion.1
  343.9 8.2 multiply_reduce_fusion.5
  359.4 8.0 fusion.231
  367.5 9.8 multiply_reduce_fusion.1
  377.2 7.3 multiply_convert_fusion.1
  404.9 21.2 %convert_reduce_fusion = (f32[3072]{0:T(1024)}, bf16[512,3072]{1,0:T(8,128)(2,1)S(1)}) fusion(bf16[1,3072,768]{2,1,0:T(8,128)(2,1)S(1)} %bitcast.429, f32[512,768]{1,0:T(8,128)S(1)} %get-tuple-element.216, f32[512,3072]{1,0:T(8,128)} %copy-done.160, f32[512,3072]{1,0:T(8,128)} %get-tuple-element.306, f32[3072]{0:T(1024)S(1)} %bitcast.436, pred[]{:T(512)S(6)} %eq.169), kind=kOutput, calls=%fused_computation.51 | convolution fusion | flops 2537419776 | bytes 22044672 | tf_op jit(solution)/shard_map/dot_general | solution.py:33
  443.0 13.6 multiply_reduce_fusion
  456.7 7.3 multiply_convert_fusion
  474.7 10.4 multiply_add_fusion.2
  493.8 10.5 multiply_add_fusion.1
  504.6 7.0 fusion.105
  511.7 6.5 fusion.106
  518.2 20.2 %multiply_add_fusion = f32[3072,768]{1,0:T(8,128)} fusion(f32[3072,768]{1,0:T(8,128)S(1)} %fusion.106, f32[3072,768]{1,0:T(8,128)S(1)} %fusion.105, f32[]{:T(128)S(6)} %convert_element_type.387, f32[]{:T(128)S(6)} %convert_element_type.386, f32[]{:T(128)S(6)} %convert_element_type.385, f32[512,768]{1,0:T(8,128)S(1)} %copy-done.64, ...), kind=kOutput, calls=%fused_computation.30 | convolution fusion | flops 2535063552 | bytes 42479628 | tf_op jit(solution)/shard_map/dot_general | solution.py:27
  538.5 36.8 %reduce-scatter.7.cloned.1.call-done = f32[48,768]{1,0:T(8,128)} async-done(((f32[768,768]{1,0:T(8,128)}), f32[48,768]{1,0:T(8,128)}) %reduce-scatter.7.cloned.1.call-update) | async-done | bytes 147472 | tf_op jit(solution)/shard_map/reduce_scatter | solution.py:331
  576.9 154.7 %reduce-scatter.5.cloned.1.call-done = f32[48,2304]{1,0:T(8,128)} async-done(((f32[768,2304]{1,0:T(8,128)}), f32[48,2304]{1,0:T(8,128)}) %reduce-scatter.5.cloned.1.call-update) | async-done | bytes 442384 | tf_op jit(solution)/shard_map/reduce_scatter | solution.py:330
  733.4 175.2 %reduce-scatter.9.cloned.1.call-done = f32[48,3072]{1,0:T(8,128)} async-done(((f32[768,3072]{1,0:T(8,128)}), f32[48,3072]{1,0:T(8,128)}) %reduce-scatter.9.cloned.1.call-update) | async-done | bytes 589840 | tf_op jit(solution)/shard_map/reduce_scatter | solution.py:332
  917.5 167.0 %reduce-scatter.11.cloned.1.call-done = f32[192,768]{1,0:T(8,128)} async-done(((f32[3072,768]{1,0:T(8,128)}), f32[192,768]{1,0:T(8,128)}) %reduce-scatter.11.cloned.1.call-update) | async-done | bytes 589840 | tf_op jit(solution)/shard_map/reduce_scatter | solution.py:333
  1125.4 77.1 %all-reduce = (f32[1,2,768]{2,1,0:T(2,128)}, f32[1,768]{1,0:T(1,128)}, f32[1,2,768]{2,1,0:T(2,128)}, f32[1,2,768]{2,1,0:T(2,128)}, f32[1,3072]{1,0:T(1,128)}, /*index=5*/f32[1,768]{1,0:T(1,128)}, f32[3]{0:T(128)}, f32[]{:T(128)}) all-reduce(f32[1,2,768]{2,1,0:T(2,128)} %fusion.326, ...), channel_id=1, replica_groups=mesh['section'=2,'dp'=16] {'dp'}, use_global_device_ids=true, to_apply=%region_37.38 | all-reduce | flops 9220 | bytes 73760 | tf_op jit(solution)/shard_map/psum | solution.py:349
  1222.1 77.3 %all-gather.9.cloned.1.call-done = bf16[768,3072]{1,0:T(8,128)(2,1)} async-done(((bf16[48,3072]{1,0:T(8,128)(2,1)}), bf16[768,3072]{1,0:T(8,128)(2,1)}) %all-gather.9.cloned.1.call-update) | async-done | bytes 4718608 | tf_op jit(solution)/shard_map/all_gather | solution.py:342
  1299.4 7.4 bitcast_convert_fusion.1
  1306.8 74.9 %all-gather.11.cloned.1.call-done = bf16[3072,768]{1,0:T(8,128)(2,1)} async-done(((bf16[192,768]{1,0:T(8,128)(2,1)}), bf16[3072,768]{1,0:T(8,128)(2,1)}) %all-gather.11.cloned.1.call-update) | async-done | bytes 4718608 | tf_op jit(solution)/shard_map/all_gather | solution.py:345
  1381.7 6.8 bitcast_convert_fusion
  (562 shorter events, 319.6 us)
Async XLA Ops:
  7.2 568.1 %reduce-scatter.7.cloned.1.call-start = ((), (), s32[]{:S(2)}) async-start(), calls=%async_computation.6 | async-start | bytes 2506752 | tf_op jit(solution)/shard_map/reduce_scatter | solution.py:331
  41.6 93.2 %copy-start.88 = (f32[768]{0:T(1024)}, f32[768]{0:T(1024)S(1)}, u32[]{:S(2)}) copy-start(f32[768]{0:T(1024)S(1)} %get-tuple-element.188) | copy-start | bytes 9220
  41.6 102.1 %copy-start.81 = (f32[768]{0:T(1024)}, f32[768]{0:T(1024)S(1)}, u32[]{:S(2)}) copy-start(f32[768]{0:T(1024)S(1)} %get-tuple-element.330) | copy-start | bytes 9220
  41.6 188.4 %copy-start.70 = (f32[768]{0:T(1024)}, f32[768]{0:T(1024)S(1)}, u32[]{:S(2)}) copy-start(f32[768]{0:T(1024)S(1)} %get-tuple-element.189) | copy-start | bytes 9220
  47.5 22.1 %copy-start.161 = (f32[512,3072]{1,0:T(8,128)}, f32[512,3072]{1,0:T(8,128)S(1)}, u32[]{:S(2)}) copy-start(f32[512,3072]{1,0:T(8,128)S(1)} %fusion.91) | copy-start | bytes 18874372
  47.6 30.9 %copy-start.109 = (s32[1,512]{1,0:T(1,128)S(1)}, s32[1,512]{1,0:T(1,128)}, u32[]{:S(2)}) copy-start(s32[1,512]{1,0:T(1,128)} %get-tuple-element.278) | copy-start | bytes 6148
  47.6 31.8 %copy-start.108 = (s32[1,512]{1,0:T(1,128)S(1)}, s32[1,512]{1,0:T(1,128)}, u32[]{:S(2)}) copy-start(s32[1,512]{1,0:T(1,128)} %get-tuple-element.277) | copy-start | bytes 6148
  75.2 10.1 collective-permute-start
  138.3 9.2 collective-permute-start.1
  175.0 34.6 %copy-start.37 = (f32[512,768]{1,0:T(8,128)}, f32[512,768]{1,0:T(8,128)S(1)}, u32[]{:S(2)}) copy-start(f32[512,768]{1,0:T(8,128)S(1)} %get-tuple-element.242) | copy-start | bytes 4718596
  175.0 55.0 %copy-start.135 = (f32[512]{0:T(512)}, f32[512]{0:T(512)S(1)}, u32[]{:S(2)}) copy-start(f32[512]{0:T(512)S(1)} %broadcast_multiply_fusion.25) | copy-start | bytes 6148
  176.1 53.9 %copy-start.148 = (f32[512]{0:T(512)}, f32[512]{0:T(512)S(1)}, u32[]{:S(2)}) copy-start(f32[512]{0:T(512)S(1)} %get-tuple-element.284) | copy-start | bytes 6148
  176.1 33.5 %copy-start.27 = (f32[512,768]{1,0:T(8,128)S(1)}, f32[512,768]{1,0:T(8,128)}, u32[]{:S(2)}) copy-start(f32[512,768]{1,0:T(8,128)} %get-tuple-element.212) | copy-start | bytes 4718596
  292.5 36.9 %collective-permute-start.2 = (bf16[512,768]{1,0:T(8,128)(2,1)}, bf16[512,768]{1,0:T(8,128)(2,1)}, u32[]{:S(2)}, u32[]{:S(2)}) collective-permute-start(bf16[512,768]{1,0:T(8,128)(2,1)} %get-tuple-element.312), channel_id=1, source_target_pairs={{16,0},{17,1},{18,2},{19,3},{20,4},{21,5},{22,6},{23,7},{24,8},{25... | collective-permute-start | bytes 2359304 | tf_op jit(solution)/shard_map/ppermute | solution.py:19
  392.1 8.7 collective-permute-start.3
  400.8 25.3 %slice-start.14 = ((s8[4718592]{0:T(1024)(128)(4,1)}), s8[4194304]{0:T(1024)(128)(4,1)S(1)}, s32[]{:S(2)}) async-start(s8[4718592]{0:T(1024)(128)(4,1)} %bitcast.430), calls=%async_computation.26 | async-start | bytes 8388608
  404.8 21.3 %copy-start.63 = (f32[512,768]{1,0:T(8,128)}, f32[512,768]{1,0:T(8,128)S(1)}, u32[]{:S(2)}) copy-start(f32[512,768]{1,0:T(8,128)S(1)} %get-tuple-element.216) | copy-start | bytes 4718596
  404.8 21.3 %copy-start.36 = (f32[512,768]{1,0:T(8,128)S(1)}, f32[512,768]{1,0:T(8,128)}, u32[]{:S(2)}) copy-start(f32[512,768]{1,0:T(8,128)} %copy-done.35) | copy-start | bytes 4718596
  404.8 21.2 %copy-start.39 = (f32[512,768]{1,0:T(8,128)S(1)}, f32[512,768]{1,0:T(8,128)}, u32[]{:S(2)}) copy-start(f32[512,768]{1,0:T(8,128)} %copy-done.37) | copy-start | bytes 4718596
  404.8 21.2 %copy-start.130 = (f32[512]{0:T(512)S(1)}, f32[512]{0:T(512)}, u32[]{:S(2)}) copy-start(f32[512]{0:T(512)} %copy-done.128) | copy-start | bytes 6148
  404.8 21.2 %copy-start.137 = (f32[512]{0:T(512)S(1)}, f32[512]{0:T(512)}, u32[]{:S(2)}) copy-start(f32[512]{0:T(512)} %copy-done.135) | copy-start | bytes 6148
  404.9 21.2 %copy-start.144 = (f32[512]{0:T(512)S(1)}, f32[512]{0:T(512)}, u32[]{:S(2)}) copy-start(f32[512]{0:T(512)} %copy-done.142) | copy-start | bytes 6148
  404.9 21.2 %copy-start.150 = (f32[512]{0:T(512)S(1)}, f32[512]{0:T(512)}, u32[]{:S(2)}) copy-start(f32[512]{0:T(512)} %copy-done.148) | copy-start | bytes 6148
  442.9 288.7 %reduce-scatter.5.cloned.1.call-start = ((), (), s32[]{:S(2)}) async-start(), calls=%async_computation.4 | async-start | bytes 7520256 | tf_op jit(solution)/shard_map/reduce_scatter | solution.py:330
  485.2 423.4 %reduce-scatter.9.cloned.1.call-start = ((), (), s32[]{:S(2)}) async-start(), calls=%async_computation.8 | async-start | bytes 10027008 | tf_op jit(solution)/shard_map/reduce_scatter | solution.py:332
  504.3 580.2 %reduce-scatter.11.cloned.1.call-start = ((), (), s32[]{:S(2)}) async-start(), calls=%async_computation.10 | async-start | bytes 10027008 | tf_op jit(solution)/shard_map/reduce_scatter | solution.py:333
  538.4 374.6 %copy-start.139 = (s32[2]{0:T(128)S(1)}, s32[2]{0:T(128)}, u32[]{:S(2)}) copy-start(s32[2]{0:T(128)} %param.42) | copy-start | bytes 28
  538.4 375.3 %copy-start.119 = (f32[768]{0:T(1024)S(1)}, f32[768]{0:T(1024)}, u32[]{:S(2)}) copy-start(f32[768]{0:T(1024)} %get-tuple-element.167) | copy-start | bytes 9220
  538.4 674.5 %all-gather.7.cloned.1.call-start = ((), (), s32[]{:S(2)}) async-start(), calls=%async_computation.7 | async-start | bytes 1253376 | tf_op jit(solution)/shard_map/all_gather | solution.py:339
  576.9 639.8 %all-gather.5.cloned.1.call-start = ((), (), s32[]{:S(2)}) async-start(), calls=%async_computation.5 | async-start | bytes 3760128 | tf_op jit(solution)/shard_map/all_gather | solution.py:336
  733.3 566.1 %all-gather.9.cloned.1.call-start = ((), (), s32[]{:S(2)}) async-start(), calls=%async_computation.9 | async-start | bytes 5013504 | tf_op jit(solution)/shard_map/all_gather | solution.py:342
  910.4 471.3 %all-gather.11.cloned.1.call-start = ((), (), s32[]{:S(2)}) async-start(), calls=%async_computation.11 | async-start | bytes 5013504 | tf_op jit(solution)/shard_map/all_gather | solution.py:345
  (159 other events, 1130.5 us)
Sparse Core Ops, SparseCore 0:
  443.0 132.1 reduce-scatter.6
  582.0 149.5 reduce-scatter.4
  738.8 169.7 reduce-scatter.8
  914.7 169.8 reduce-scatter.10
  1087.6 55.1 all-gather.6
  1146.4 70.1 all-gather.4
  1220.4 79.0 all-gather.8
  1302.6 79.0 all-gather.10
where the time goes:
time: 1410 us; the launch traced here: 1400 us
  waiting for transfers between devices  687 us (49%)
  matrix products  392 us (28%)
  other arithmetic  144 us (10%)
  blocking collectives  77.1 us (5%)
  local copies, waits for them, and re-layouts  70 us (5%)
  between operations  17.3 us (1%)
    reduce_scatter x1, waiting for transfers between devices, local(): lax.psum_scatter(grads[6], 'dp', scatter_dimension=0, tiled=True)  175 us
    reduce_scatter x1, waiting for transfers between devices, local(): lax.psum_scatter(grads[8], 'dp', scatter_dimension=0, tiled=True)  167 us
    reduce_scatter x1, waiting for transfers between devices, local(): lax.psum_scatter(grads[0], 'dp', scatter_dimension=0, tiled=True)  155 us
    dot_general x12, matrix products, matmul(): return jnp.dot(left, right, preferred_element_type=jnp.float32)  124 us
    dot_general x12, matrix products, matmul_left_t(): lax.dot_general(left, right, (((0,), (0,)), ((), ())), preferred_element_...  84.2 us
    dot_general x12, matrix products, matmul_right_t(): lax.dot_general(left, right, (((1,), (1,)), ((), ())), preferred_element_...  79 us
    all_gather x1, waiting for transfers between devices, local(): lax.all_gather(big_shards[2].astype(jnp.bfloat16), 'dp', axis=0, tiled=True)  77.3 us
    psum x1, blocking collectives, local(): lax.psum((grads[1], grads[3], grads[4], grads[5], grads[7], grads[9]), 'dp')  77.1 us
  transfers between devices with their start and end apart: 12, of which 7 were waited for; matrix products, arithmetic and copies ran while one was open for 16% of the time, Pallas kernels for 0%

commit v1 on v0

v1 whole, which is shorter than its diff:
```python
import functools

import jax
import jax.numpy as jnp
from jax import lax
from jax.experimental import pallas as pl
from jax.experimental.pallas import tpu as pltpu
from jax.sharding import PartitionSpec as P

HEADS = 12
HEAD_DIM = 64
EPSILON = 1e-12
MASKED = -1e30
F32 = jnp.float32
BF16 = jnp.bfloat16
MIB = 2**20
SAVED = ("qkv", "e", "rinv", "mixed", "xhat1", "r", "firstb", "act", "slope", "xhat2")
ANY = pl.BlockSpec(memory_space=pl.ANY)
VMEM = pl.BlockSpec(memory_space=pltpu.VMEM)
SMEM = pl.BlockSpec(memory_space=pltpu.SMEM)


def mm(left, right):
    return jnp.dot(left, right, preferred_element_type=F32)


def mm_left_t(left, right):
    return lax.dot_general(left, right, (((0,), (0,)), ((), ())), preferred_element_type=F32)


def mm_right_t(left, right):
    return lax.dot_general(left, right, (((1,), (1,)), ((), ())), preferred_element_type=F32)


def lanes(start, size):
    return pl.ds(pl.multiple_of(start, size), size)


def gelu_and_slope(v):
    z = jnp.abs(v) * 0.7071067811865476
    t = 1.0 / (1.0 + 0.3275911 * z)
    e = jnp.exp(-0.5 * v * v)
    poly = t * (
        0.127414796 + t * (-0.142248368 + t * (0.7107068705 + t * (-0.7265760135 + t * 0.5307027145)))
    )
    tail = poly * e
    cdf = jnp.where(v >= 0, 1.0 - tail, tail)
    return v * cdf, cdf + v * e * 0.3989422804014327


def start_from(flag, pairs):
    for own, peer, target, sem in pairs:

        @pl.when(flag == 1)
        def _(own=own, target=target, sem=sem):
            pltpu.make_async_copy(own, target, sem).start()

        @pl.when(flag == 0)
        def _(peer=peer, target=target, sem=sem):
            pltpu.make_async_copy(peer, target, sem).start()


def forward_kernel(
    flags, cls_at, vec_own, vec_peer, seg_cols, seg_rows, h_any,
    win_own, wout_own, wid_own, nar_own, win_peer, wout_peer, wid_peer, nar_peer,
    qkv_o, e_o, rinv_o, mixed_o, xhat1_o, r_o, firstb_o, act_o, slope_o, xhat2_o, xb_o, small_o,
    h, win, wout, wid, nar, bias, qkv, e_v, rinv, mixed, xhat1, rr, first, firstb, act, slope, xhat2, xb, feed, vec,
    sems, out_sems,
):
    flag, row, valid, h_row = flags[0], flags[1], flags[2], flags[3]
    length, width = h.shape
    ff = wid.shape[1]
    start_from(flag, [
        (win_own, win_peer, win, sems.at[0]),
        (wout_own, wout_peer, wout, sems.at[1]),
        (wid_own, wid_peer, wid, sems.at[2]),
        (nar_own, nar_peer, nar, sems.at[3]),
    ])
    load_h = pltpu.make_async_copy(h_any.at[h_row], h, sems.at[4])
    load_h.start()
    stores = []

    def put(source, target):
        copy = pltpu.make_async_copy(source, target, out_sems.at[len(stores)])
        copy.start()
        stores.append(copy)

    vec[...] = jnp.where(flag == 1, vec_own[...], vec_peer[...])
    bias[...] = jnp.where(seg_cols[row][:, :1] == seg_rows[pl.ds(row, 1), :], 0.0, MASKED)
    load_h.wait()
    pltpu.make_async_copy(win_own, win, sems.at[0]).wait()

    tile = 256
    for part in range(3):
        shift = [vec[0:1, :], None, vec[1:2, :]][part]
        for j in range(width // tile):
            at = part * width + j * tile
            got = mm(h[...], win[:, at : at + tile])
            if shift is not None:
                got = got + shift[:, j * tile : (j + 1) * tile]
            got = got.astype(BF16)
            if part == 0:
                got = got * BF16(HEAD_DIM**-0.5)
            qkv[:, at : at + tile] = got
    put(qkv, qkv_o)

    low = lax.broadcasted_iota(jnp.int32, (length, 128), 1) < HEAD_DIM
    ones = jnp.ones((length, 128), BF16)

    def pair(p, carry):
        q = qkv[:, lanes(p * 128, 128)]
        k = qkv[:, lanes(width + p * 128, 128)]
        v = qkv[:, lanes(2 * width + p * 128, 128)]
        v1 = jnp.concatenate([v, ones], axis=1)
        outs = []
        for i in range(2):
            qm = jnp.where(low if i == 0 else ~low, q, BF16(0))
            s = mm_right_t(qm, k) + bias[...]
            top = jnp.max(s, axis=1, keepdims=True)
            e = jnp.exp(s - top).astype(BF16)
            e_v[2 * p + i] = e
            outs.append(mm(e, v1))
        r0 = 1.0 / outs[0][:, 128:]
        r1 = 1.0 / outs[1][:, 128:]
        m = jnp.where(low, outs[0][:, :128] * r0, outs[1][:, :128] * r1)
        mixed[:, lanes(p * 128, 128)] = m.astype(BF16)
        rinv[:, lanes(p * 128, 128)] = jnp.where(low, r0, r1)
        return carry

    lax.fori_loop(0, HEADS // 2, pair, 0)
    put(e_v, e_o)
    put(rinv, rinv_o)
    put(mixed, mixed_o)

    pltpu.make_async_copy(wout_own, wout, sems.at[1]).wait()
    block = 128
    sums = jnp.zeros((3, width), F32)

    def norm_first(b, total):
        rows = pl.ds(pl.multiple_of(b * block, block), block)
        ok = (lax.broadcasted_iota(jnp.int32, (block, 1), 0) + b * block < valid).astype(F32)
        branch = mm(mixed[rows, :], wout[...]) + vec[2:3, :]
        u = h[rows, :].astype(F32) + branch
        c = u - jnp.mean(u, axis=1, keepdims=True)
        f = lax.rsqrt(jnp.mean(c * c, axis=1, keepdims=True) + EPSILON)
        x = c * f
        xhat1[rows, :] = x
        rr[0, rows, :] = jnp.broadcast_to(f, (block, 128))
        y = x * vec[3:4, :] + vec[5:6, :]
        first[rows, :] = y
        firstb[rows, :] = y.astype(BF16)
        return total + jnp.sum(ok * branch * branch, axis=0, keepdims=True)

    branch_sum = lax.fori_loop(0, length // block, norm_first, jnp.zeros((1, width), F32))
    put(xhat1, xhat1_o)
    put(firstb, firstb_o)

    pltpu.make_async_copy(wid_own, wid, sems.at[2]).wait()
    pltpu.make_async_copy(nar_own, nar, sems.at[3]).wait()
    feed[...] = jnp.broadcast_to(vec[11:12, :], feed.shape)

    def widen(j):
        at = j * tile
        hid = mm(firstb[...], wid[:, lanes(at, tile)]) + vec[pl.ds(12 + j, 1), 0:tile]
        a, d = gelu_and_slope(hid)
        act[:, lanes(at, tile)] = a.astype(BF16)
        slope[:, lanes(at, tile)] = d.astype(BF16)

    def narrow(j):
        feed[...] += mm(act[:, lanes(j * tile, tile)], nar[lanes(j * tile, tile), :])

    widen(0)

    def ffn(j, carry):
        narrow(j - 1)
        widen(j)
        return carry

    lax.fori_loop(1, ff // tile, ffn, 0)
    put(act, act_o)
    put(slope, slope_o)
    narrow(ff // tile - 1)

    def norm_second(b, totals):
        rows = pl.ds(pl.multiple_of(b * block, block), block)
        ok = (lax.broadcasted_iota(jnp.int32, (block, 1), 0) + b * block < valid).astype(F32)
        fd = feed[rows, :]
        u = first[rows, :] + fd
        c = u - jnp.mean(u, axis=1, keepdims=True)
        f = lax.rsqrt(jnp.mean(c * c, axis=1, keepdims=True) + EPSILON)
        x = c * f
        xhat2[rows, :] = x
        rr[1, rows, :] = jnp.broadcast_to(f, (block, 128))
        y = x * vec[4:5, :] + vec[6:7, :]
        first[rows, :] = y
        xb[rows, :] = y.astype(BF16)
        return (
            totals[0] + jnp.sum(ok * u * u, axis=0, keepdims=True),
            totals[1] + jnp.sum(ok * fd * fd, axis=0, keepdims=True),
        )

    zero = jnp.zeros((1, width), F32)
    stream_sum, feed_sum = lax.fori_loop(0, length // block, norm_second, (zero, zero))
    put(xhat2, xhat2_o)
    put(rr, r_o)
    put(xb, xb_o)
    for i in range(8):
        small_o[i : i + 1, :] = first[pl.ds(cls_at[i], 1), :]
    small_o[8:9, :] = stream_sum
    small_o[9:10, :] = branch_sum
    small_o[10:11, :] = feed_sum
    small_o[11:16, :] = jnp.zeros((5, width), F32)
    for copy in stores:
        copy.wait()


def forward(flags, cls_at, vecs, seg_cols, seg_rows, h, own, peer):
    length = seg_rows.shape[1]
    width = h.shape[-1]
    ff = own[2].shape[1]
    saved = [
        ((length, 3 * width), BF16), ((HEADS, length, length), BF16), ((length, width), F32), ((length, width), BF16),
        ((length, width), F32), ((2, length, 128), F32), ((length, width), BF16), ((length, ff), BF16),
        ((length, ff), BF16), ((length, width), F32), ((length, width), BF16),
    ]
    names = (*SAVED, "xb")
    out = pl.pallas_call(
        forward_kernel,
        out_shape=[jax.ShapeDtypeStruct(s, d) for s, d in saved] + [jax.ShapeDtypeStruct((16, width), F32)],
        in_specs=[SMEM, SMEM, VMEM, VMEM, VMEM, VMEM] + [ANY] * 9,
        out_specs=[ANY] * len(saved) + [VMEM],
        scratch_shapes=[
            pltpu.VMEM((length, width), BF16),
            *[pltpu.VMEM(w.shape, BF16) for w in own],
            pltpu.VMEM((length, length), F32),
            pltpu.VMEM((length, 3 * width), BF16),
            pltpu.VMEM((HEADS, length, length), BF16),
            pltpu.VMEM((length, width), F32),
            pltpu.VMEM((length, width), BF16),
            pltpu.VMEM((length, width), F32),
            pltpu.VMEM((2, length, 128), F32),
            pltpu.VMEM((length, width), F32),
            pltpu.VMEM((length, width), BF16),
            pltpu.VMEM((length, ff), BF16),
            pltpu.VMEM((length, ff), BF16),
            pltpu.VMEM((length, width), F32),
            pltpu.VMEM((length, width), BF16),
            pltpu.VMEM((length, width), F32),
            pltpu.VMEM(vecs[0].shape, F32),
            pltpu.SemaphoreType.DMA((5,)),
            pltpu.SemaphoreType.DMA((11,)),
        ],
        compiler_params=pltpu.CompilerParams(vmem_limit_bytes=60 * MIB),
        cost_estimate=pl.CostEstimate(flops=9 * 10**9, bytes_accessed=40 * 10**6, transcendentals=5 * 10**6),
        name="forward_layer",
    )(flags, cls_at, vecs[0], vecs[1], seg_cols, seg_rows, h, *own, *peer)
    return dict(zip(names, out[:-1])), out[-1]


def backward_kernel(
    flags, vec_own, vec_peer, g_any, h_any, qkv_a, e_a, rinv_a, mixed_a, xhat1_a, r_a, firstb_a, act_a, slope_a, xhat2_a,
    win_own, wout_own, wid_own, nar_own, win_peer, wout_peer, wid_peer, nar_peer,
    grad_o, din_o, dinb_o, small_o,
    g, h, win, wout, wid, nar, qkv, e_v, rinv, mixed, xhat1, rr, firstb, act, slope, xhat2,
    vec, ds, dfeed, dh, dres, dbr, dm, dqkv, dinb, row_stage, col_stage, wbias,
    sems, e_sems, stage_sems, out_sems,
):
    flag, g_row, h_row = flags[0], flags[1], flags[2]
    length, width = h.shape
    ff = wid.shape[1]
    tile = 256
    block = 128
    loads = {}

    def load(name, source, target, i):
        loads[name] = pltpu.make_async_copy(source, target, sems.at[i])
        loads[name].start()

    load("g", g_any.at[g_row], g, 4)
    load("xhat2", xhat2_a, xhat2, 5)
    load("r", r_a, rr, 6)
    start_from(flag, [(nar_own, nar_peer, nar, sems.at[3])])
    load("act", act_a, act, 7)
    load("slope", slope_a, slope, 8)
    load("firstb", firstb_a, firstb, 9)
    start_from(flag, [(wid_own, wid_peer, wid, sems.at[2])])
    load("xhat1", xhat1_a, xhat1, 10)
    load("mixed", mixed_a, mixed, 11)
    start_from(flag, [(wout_own, wout_peer, wout, sems.at[1])])
    load("rinv", rinv_a, rinv, 12)
    load("qkv", qkv_a, qkv, 13)

    def load_e(p, slot):
        return pltpu.make_async_copy(e_a.at[pl.ds(2 * p, 2)], e_v.at[slot], e_sems.at[slot])

    load_e(0, 0).start()
    load("h", h_any.at[h_row], h, 14)
    start_from(flag, [(win_own, win_peer, win, sems.at[0])])

    vec[...] = jnp.where(flag == 1, vec_own[...], vec_peer[...])
    zero = jnp.zeros((1, width), F32)

    def norm_back(up, x, f):
        return f * (up - jnp.mean(up, axis=1, keepdims=True) - x * jnp.mean(up * x, axis=1, keepdims=True))

    loads["g"].wait()
    loads["xhat2"].wait()
    loads["r"].wait()

    def second(b, sums):
        rows = pl.ds(pl.multiple_of(b * block, block), block)
        up = g[rows, :].astype(F32)
        x = xhat2[rows, :]
        d = norm_back(up * vec[4:5, :], x, rr[1, rows, 0:1])
        ds[rows, :] = d
        db = d.astype(BF16)
        dfeed[rows, :] = db
        return (
            sums[0] + jnp.sum(up * x, axis=0, keepdims=True),
            sums[1] + jnp.sum(up, axis=0, keepdims=True),
            sums[2] + jnp.sum(db.astype(F32), axis=0, keepdims=True),
        )

    gain2, shift2, narrow_bias = lax.fori_loop(0, length // block, second, (zero, zero, zero))

    def stage_rows(n, value, target, first):
        slot = n % 2
        @pl.when(jnp.logical_not(first))
        def _():
            pltpu.make_async_copy(row_stage.at[slot], target, stage_sems.at[slot]).wait()
        row_stage[slot] = value.astype(BF16)
        pltpu.make_async_copy(row_stage.at[slot], target, stage_sems.at[slot]).start()

    def stage_cols(n, value, target, first):
        slot = n % 2
        @pl.when(jnp.logical_not(first))
        def _():
            pltpu.make_async_copy(col_stage.at[slot], target, stage_sems.at[2 + slot]).wait()
        col_stage[slot] = value.astype(BF16)
        pltpu.make_async_copy(col_stage.at[slot], target, stage_sems.at[2 + slot]).start()

    pltpu.make_async_copy(nar_own, nar, sems.at[3]).wait()
    loads["act"].wait()
    loads["slope"].wait()
    loads["firstb"].wait()

    def ffn(j, carry):
        at = lanes(j * tile, tile)
        da = mm_right_t(dfeed[...], nar[at, :])
        d = (slope[:, at].astype(F32) * da).astype(BF16)
        dh[:, at] = d
        wbias[pl.ds(j, 1), :] = jnp.sum(d.astype(F32), axis=0, keepdims=True)
        stage_rows(j, mm_left_t(act[:, at], dfeed[...]), grad_o.at[8 + j // 3, lanes((j % 3) * tile, tile), :], j < 2)
        stage_cols(j, mm_left_t(firstb[...], d), grad_o.at[4 + j // 3, :, lanes((j % 3) * tile, tile)], j < 2)
        return carry

    lax.fori_loop(0, ff // tile, ffn, 0)
    pltpu.make_async_copy(wid_own, wid, sems.at[2]).wait()

    def first_grad(j, carry):
        at = lanes(j * tile, tile)
        ds[:, at] = ds[:, at] + mm_right_t(dh[...], wid[at, :])
        return carry

    lax.fori_loop(0, width // tile, first_grad, 0)

    loads["xhat1"].wait()

    def first(b, sums):
        rows = pl.ds(pl.multiple_of(b * block, block), block)
        up = ds[rows, :]
        x = xhat1[rows, :]
        d = norm_back(up * vec[3:4, :], x, rr[0, rows, 0:1])
        dres[rows, :] = d
        db = d.astype(BF16)
        dbr[rows, :] = db
        return (
            sums[0] + jnp.sum(up * x, axis=0, keepdims=True),
            sums[1] + jnp.sum(up, axis=0, keepdims=True),
            sums[2] + jnp.sum(db.astype(F32), axis=0, keepdims=True),
        )

    gain1, shift1, out_shift = lax.fori_loop(0, length // block, first, (zero, zero, zero))

    loads["mixed"].wait()
    pltpu.make_async_copy(wout_own, wout, sems.at[1]).wait()
    loads["rinv"].wait()
    loads["qkv"].wait()

    def out_grad(j, carry):
        at = lanes(j * tile, tile)
        stage_cols(j, mm_left_t(mixed[...], dbr[:, at]), grad_o.at[3, :, at], j < 0)
        d = mm_right_t(dbr[...], wout[at, :]).astype(BF16).astype(F32)
        dm[:, at] = (d * rinv[:, at]).astype(BF16)
        return carry

    lax.fori_loop(0, width // tile, out_grad, 0)

    low = lax.broadcasted_iota(jnp.int32, (length, 128), 1) < HEAD_DIM

    def pair(p, carry):
        slot = p % 2
        @pl.when(p + 1 < HEADS // 2)
        def _():
            load_e(p + 1, 1 - slot).start()
        at_q, at_k, at_v = lanes(p * 128, 128), lanes(width + p * 128, 128), lanes(2 * width + p * 128, 128)
        q, k, v = qkv[:, at_q], qkv[:, at_k], qkv[:, at_v]
        d = dm[:, at_q]
        prod = d.astype(F32) * mixed[:, at_q].astype(F32)
        load_e(p, slot).wait()
        dq, dk, dv = [], [], []
        for i in range(2):
            mine = low if i == 0 else ~low
            delta = jnp.sum(jnp.where(mine, prod, 0.0), axis=1, keepdims=True)
            dp = mm_right_t(jnp.where(mine, d, BF16(0)), v)
            e = e_v[slot, i]
            s = (e.astype(F32) * (dp - delta)).astype(BF16)
            dq.append(mm(s, k))
            dk.append(mm_left_t(s, q))
            dv.append(mm_left_t(e, d))
        dqkv[:, at_q] = (jnp.where(low, dq[0], dq[1]) * HEAD_DIM**-0.5).astype(BF16)
        dqkv[:, at_k] = jnp.where(low, dk[0], dk[1]).astype(BF16)
        dqkv[:, at_v] = jnp.where(low, dv[0], dv[1]).astype(BF16)
        return carry

    lax.fori_loop(0, HEADS // 2, pair, 0)

    loads["h"].wait()

    def in_grad(j, carry):
        at = lanes(j * tile, tile)
        stage_cols(j + 1, mm_left_t(h[...], dqkv[:, at]), grad_o.at[j // 3, :, lanes((j % 3) * tile, tile)], j < 0)
        return carry

    lax.fori_loop(0, 3 * width // tile, in_grad, 0)
    pltpu.make_async_copy(win_own, win, sems.at[0]).wait()

    def input_grad(j, carry):
        at = lanes(j * tile, tile)
        d = dres[:, at] + mm_right_t(dqkv[...], win[at, :])
        dres[:, at] = d
        dinb[:, at] = d.astype(BF16)
        return carry

    lax.fori_loop(0, width // tile, input_grad, 0)
    out_f = pltpu.make_async_copy(dres, din_o, out_sems.at[0])
    out_b = pltpu.make_async_copy(dinb, dinb_o.at[0], out_sems.at[1])
    out_f.start()
    out_b.start()
    small_o[0:1, :] = jnp.sum(dqkv[:, 0:width].astype(F32), axis=0, keepdims=True)
    small_o[1:2, :] = jnp.sum(dqkv[:, 2 * width :].astype(F32), axis=0, keepdims=True)
    small_o[2:3, :] = out_shift
    small_o[3:4, :] = gain1
    small_o[4:5, :] = gain2
    small_o[5:6, :] = shift1
    small_o[6:7, :] = shift2
    for i in range(ff // tile):
        small_o[7 + i // 3 : 8 + i // 3, (i % 3) * tile : (i % 3 + 1) * tile] = wbias[i : i + 1, :]
    small_o[11:12, :] = narrow_bias
    small_o[12:16, :] = jnp.zeros((4, width), F32)
    for slot in range(2):
        pltpu.make_async_copy(row_stage.at[slot], grad_o.at[8, 0:tile, :], stage_sems.at[slot]).wait()
        pltpu.make_async_copy(col_stage.at[slot], grad_o.at[0, :, 0:tile], stage_sems.at[2 + slot]).wait()
    out_f.wait()
    out_b.wait()


def backward(flags, vecs, g, h, saved, own, peer):
    length, width = saved["xhat1"].shape
    ff = own[2].shape[1]
    return pl.pallas_call(
        backward_kernel,
        out_shape=[
            jax.ShapeDtypeStruct((12, width, width), BF16),
            jax.ShapeDtypeStruct((length, width), F32),
            jax.ShapeDtypeStruct((1, length, width), BF16),
            jax.ShapeDtypeStruct((16, width), F32),
        ],
        in_specs=[SMEM, VMEM, VMEM] + [ANY] * 20,
        out_specs=[ANY, ANY, ANY, VMEM],
        scratch_shapes=[
            pltpu.VMEM((length, width), BF16),
            pltpu.VMEM((length, width), BF16),
            *[pltpu.VMEM(w.shape, BF16) for w in own],
            pltpu.VMEM((length, 3 * width), BF16),
            pltpu.VMEM((2, 2, length, length), BF16),
            pltpu.VMEM((length, width), F32),
            pltpu.VMEM((length, width), BF16),
            pltpu.VMEM((length, width), F32),
            pltpu.VMEM((2, length, 128), F32),
            pltpu.VMEM((length, width), BF16),
            pltpu.VMEM((length, ff), BF16),
            pltpu.VMEM((length, ff), BF16),
            pltpu.VMEM((length, width), F32),
            pltpu.VMEM(vecs[0].shape, F32),
            pltpu.VMEM((length, width), F32),
            pltpu.VMEM((length, width), BF16),
            pltpu.VMEM((length, ff), BF16),
            pltpu.VMEM((length, width), F32),
            pltpu.VMEM((length, width), BF16),
            pltpu.VMEM((length, width), BF16),
            pltpu.VMEM((length, 3 * width), BF16),
            pltpu.VMEM((length, width), BF16),
            pltpu.VMEM((2, 256, width), BF16),
            pltpu.VMEM((2, width, 256), BF16),
            pltpu.VMEM((16, 256), F32),
            pltpu.SemaphoreType.DMA((15,)),
            pltpu.SemaphoreType.DMA((2,)),
            pltpu.SemaphoreType.DMA((4,)),
            pltpu.SemaphoreType.DMA((2,)),
        ],
        compiler_params=pltpu.CompilerParams(vmem_limit_bytes=60 * MIB),
        cost_estimate=pl.CostEstimate(flops=18 * 10**9, bytes_accessed=60 * 10**6, transcendentals=0),
        name="backward_layer",
    )(flags, vecs[0], vecs[1], g, h, *[saved[n] for n in SAVED], *own, *peer)


def swap_sections(array):
    return lax.ppermute(array, "section", [(0, 1), (1, 0)])


MESH = pl.DeviceIdType.MESH


def sum_plan(devices, rows):
    side = round((devices / 2) ** (1 / 3))
    extents = [side, side, devices // (side * side)]
    axes, stride = [], 1
    for extent in extents:
        steps, step = [], 1
        while step < extent:
            steps.append(stride * step)
            step *= 2
        axes.append(steps)
        stride *= extent
    x, y, z = axes
    unit = 16 * devices if rows % (16 * devices) == 0 else 8 * devices
    units = rows // unit
    last = round(units * 2 / 9)
    head = (units - last + 1) // 2
    counts = [head, units - last - head, last]
    plan, base = [], 0
    for count, order in zip(counts, (x + y + z, y + x + z, z + x + y)):
        plan.append((base, unit, count, order))
        base += unit * count
    return plan


def halves(rows, cols, stages):
    shapes = []
    for _ in range(stages):
        by_rows = rows >= 32
        rows, cols = (rows // 2, cols) if by_rows else (rows, cols // 2)
        shapes.append((rows, cols, by_rows))
    return shapes


def sum_kernel(plan, grad0, grad1, small_in, out, small_out, total, other, small_recv, small_acc, *rest):
    stages = len(plan[0][3])
    recvs = rest[: len(plan) * stages]
    load_sems, pair_sems, rs_sems, ag_sems, out_sems, small_sems = rest[len(plan) * stages :]
    section, me = lax.axis_index("section"), lax.axis_index("dp")
    width = total.shape[1]

    def bit_of(distance):
        return lax.rem(me // distance, 2)

    def partner(distance):
        return (section, me + distance * (1 - 2 * bit_of(distance)))

    peer = (1 - section, me)

    barrier = pltpu.get_barrier_semaphore()
    pl.semaphore_signal(barrier, inc=1, device_id=peer, device_id_type=MESH)
    for distance in plan[0][3]:
        pl.semaphore_signal(barrier, inc=1, device_id=partner(distance), device_id_type=MESH)
    pl.semaphore_wait(barrier, stages + 1)

    steps = max(count for _, _, count, _ in plan)

    def rows_at(part, k):
        base, unit, _, _ = plan[part]
        return pl.ds(pl.multiple_of(base + k * unit, 16), unit)

    def load(part, k, source):
        return pltpu.make_async_copy(source.at[rows_at(part, k)], total.at[rows_at(part, k)], load_sems.at[part, k])

    def trade(part, k, source):
        return pltpu.make_async_remote_copy(
            src_ref=source.at[rows_at(part, k)], dst_ref=other.at[rows_at(part, k)],
            send_sem=pair_sems.at[0, part, k], recv_sem=pair_sems.at[1, part, k],
            device_id=peer, device_id_type=MESH,
        )

    def each(count, k, body):
        pl.when((k >= 0) & (k < count))(body)

    def begin(k, carry):
        for part, (_, _, count, _) in enumerate(plan):

            def go(part=part):
                @pl.when(section == 0)
                def _():
                    load(part, k, grad0).start()
                    trade(part, k, grad1).start()

                @pl.when(section == 1)
                def _():
                    load(part, k, grad1).start()
                    trade(part, k, grad0).start()

            each(count, k, go)
        return carry

    lax.fori_loop(0, steps, begin, 0)

    def regions(part, k, stage):
        base, unit, _, order = plan[part]
        row, col = base + k * unit, 0
        for s, (rows, cols, by_rows) in enumerate(halves(unit, width, stages)):
            bit = bit_of(order[s])
            keep, send = bit, 1 - bit
            if by_rows:
                kept, sent = (row + keep * rows, rows, col, cols), (row + send * rows, rows, col, cols)
            else:
                kept, sent = (row, rows, col + keep * cols, cols), (row, rows, col + send * cols, cols)
            if s == stage:
                return kept, sent
            row, col = kept[0], kept[2]

    def view(ref, region):
        row, rows, col, cols = region
        if cols == width:
            return ref.at[pl.ds(pl.multiple_of(row, 16), rows)]
        return ref.at[pl.ds(pl.multiple_of(row, 16), rows), pl.ds(pl.multiple_of(col, 128), cols)]

    def reduce_copy(part, k, stage):
        _, sent = regions(part, k, stage)
        return pltpu.make_async_remote_copy(
            src_ref=view(total, sent), dst_ref=recvs[part * stages + stage].at[k],
            send_sem=rs_sems.at[0, part, stage, k], recv_sem=rs_sems.at[1, part, stage, k],
            device_id=partner(plan[part][3][stage]), device_id_type=MESH,
        )

    def gather_copy(part, k, stage):
        kept, _ = regions(part, k, stage)
        return pltpu.make_async_remote_copy(
            src_ref=view(other, kept), dst_ref=view(other, kept),
            send_sem=ag_sems.at[0, part, stage, k], recv_sem=ag_sems.at[1, part, stage, k],
            device_id=partner(plan[part][3][stage]), device_id_type=MESH,
        )

    def store(part, k):
        return pltpu.make_async_copy(other.at[rows_at(part, k)], out.at[rows_at(part, k)], out_sems.at[part, k])

    def add(region, source, target=total):
        row, rows, col, cols = region
        block = min(rows, 32)

        def body(i, carry):
            at = (pl.ds(pl.multiple_of(row + i * block, 16), block), pl.ds(pl.multiple_of(col, 128), cols))
            target[at] = total[at] + source[pl.ds(pl.multiple_of(i * block, 16), block), :]
            return carry

        lax.fori_loop(0, rows // block, body, 0)

    def task(part, k, stage):
        if stage == 0:
            load(part, k, grad0).wait()
            trade(part, k, grad0).wait_recv()
            base, unit, _, _ = plan[part]
            add((base + k * unit, unit, 0, width), other.at[rows_at(part, k)])
            reduce_copy(part, k, 0).start()
        elif stage <= stages:
            reduce_copy(part, k, stage - 1).wait_recv()
            kept, _ = regions(part, k, stage - 1)
            add(kept, recvs[part * stages + stage - 1].at[k], total if stage < stages else other)
            if stage < stages:
                reduce_copy(part, k, stage).start()
            else:
                gather_copy(part, k, stages - 1).start()
        else:
            past = 2 * stages - stage
            gather_copy(part, k, past).wait_recv()
            if past > 0:
                gather_copy(part, k, past - 1).start()
            else:
                store(part, k).start()

    small_acc[0] = small_in[...]

    def small_copy(stage):
        return pltpu.make_async_remote_copy(
            src_ref=small_acc.at[stage], dst_ref=small_recv.at[stage],
            send_sem=small_sems.at[0, stage], recv_sem=small_sems.at[1, stage],
            device_id=partner(plan[0][3][stage]), device_id_type=MESH,
        )

    def small_step(stage):
        if stage > 0:
            small_copy(stage - 1).wait_recv()
            small_acc[stage] = small_acc[stage - 1] + small_recv[stage - 1]
        if stage < stages:
            small_copy(stage).start()
        else:
            small_out[...] = small_acc[stages]

    def step(t, carry):
        for stage in range(2 * stages + 1):
            for part, (_, _, count, _) in enumerate(plan):
                each(count, t - stage, lambda part=part, stage=stage: task(part, t - stage, stage))
        for stage in range(stages + 1):
            pl.when(t == stage)(lambda stage=stage: small_step(stage))
        return carry

    lax.fori_loop(0, steps + 2 * stages, step, 0)

    def finish(k, carry):
        for part, (_, _, count, _) in enumerate(plan):

            def go(part=part):
                trade(part, k, grad0).wait_send()
                for stage in range(stages):
                    reduce_copy(part, k, stage).wait_send()
                    gather_copy(part, k, stage).wait_send()
                store(part, k).wait()

            each(count, k, go)
        return carry

    lax.fori_loop(0, steps, finish, 0)
    for stage in range(stages):
        small_copy(stage).wait_send()


def sum_gradients(grad0, grad1, small):
    devices = lax.axis_size("dp")
    shape = grad0.shape
    rows, width = shape[0] * shape[1], shape[2]
    plan = sum_plan(devices, rows)
    stages = len(plan[0][3])
    steps = max(count for _, _, count, _ in plan)
    recvs = [
        pltpu.VMEM((count, r, c), BF16)
        for _, unit, count, _ in plan
        for r, c, _ in halves(unit, width, stages)
    ]
    parts = len(plan)
    blocks, small = pl.pallas_call(
        functools.partial(sum_kernel, plan),
        out_shape=[jax.ShapeDtypeStruct((rows, width), BF16), jax.ShapeDtypeStruct(small.shape, F32)],
        in_specs=[ANY, ANY, VMEM],
        out_specs=[ANY, VMEM],
        scratch_shapes=[
            pltpu.VMEM((rows, width), BF16),
            pltpu.VMEM((rows, width), BF16),
            pltpu.VMEM((stages, *small.shape), F32),
            pltpu.VMEM((stages + 1, *small.shape), F32),
            *recvs,
            pltpu.SemaphoreType.DMA((parts, steps)),
            pltpu.SemaphoreType.DMA((2, parts, steps)),
            pltpu.SemaphoreType.DMA((2, parts, stages, steps)),
            pltpu.SemaphoreType.DMA((2, parts, stages, steps)),
            pltpu.SemaphoreType.DMA((parts, steps)),
            pltpu.SemaphoreType.DMA((2, stages)),
        ],
        compiler_params=pltpu.CompilerParams(collective_id=0, has_side_effects=True, vmem_limit_bytes=60 * MIB),
        cost_estimate=pl.CostEstimate(flops=10**7, bytes_accessed=60 * 10**6, transcendentals=0),
        name="sum_gradients",
    )(grad0.reshape(rows, width), grad1.reshape(rows, width), small)
    return blocks.reshape(shape), small


def local(
    hidden_in, segment_ids, cls_positions, valid_counts, proj_in, proj_bias, proj_out, out_shift, norm_gains,
    norm_shifts, widen, widen_bias, narrow, narrow_bias, cotangent,
):
    section = lax.axis_index("section")
    row_count, length = segment_ids.shape
    width = hidden_in.shape[1]
    own = (proj_in[0], proj_out[0], widen[0], narrow[0])
    tiles = widen_bias[0].reshape(-1, 256)
    vec_own = jnp.concatenate([
        proj_bias[0], out_shift, norm_gains[0], norm_shifts[0], jnp.zeros((4, width), F32), narrow_bias,
        jnp.pad(tiles, ((0, 0), (0, width - 256))),
    ])
    peer = tuple(swap_sections(w) for w in own)
    vecs = (vec_own, swap_sections(vec_own))
    row = section
    valid = valid_counts[row]
    cls_at = cls_positions[row]
    seg_cols = jnp.broadcast_to(segment_ids[:, :, None], (row_count, length, 128))
    h0 = hidden_in.reshape(row_count, length, width)
    g1 = cotangent.reshape(row_count, length, width)
    mine = [(section == layer).astype(jnp.int32) for layer in range(2)]
    none = jnp.zeros((), jnp.int32)

    saved0, small0 = forward(
        jnp.stack([mine[0], row, valid, row]), cls_at, vecs, seg_cols, segment_ids, h0, own, peer
    )
    h1 = saved0["xb"][None]
    saved1, small1 = forward(
        jnp.stack([mine[1], row, valid, none]), cls_at, vecs, seg_cols, segment_ids, h1, own, peer
    )
    grad1, din1, dinb1, back1 = backward(jnp.stack([mine[1], row, none]), vecs, g1, h1, saved1, own, peer)
    grad0, din0, _, back0 = backward(jnp.stack([mine[0], none, row]), vecs, dinb1, h0, saved0, own, peer)

    first = section == 0
    all0 = jnp.concatenate([small0, back0])
    all1 = jnp.concatenate([small1, back1])
    kept = jnp.where(first, all0, all1)
    got = swap_sections(jnp.where(first, all1, all0))
    section_cls = jnp.where(first, jnp.stack([kept[:8], got[:8]]), jnp.stack([got[:8], kept[:8]]))
    din_kept = jnp.where(first, din0, din1)
    din_got = swap_sections(jnp.where(first, din1, din0))
    input_grads = jnp.where(first, jnp.concatenate([din_kept, din_got]), jnp.concatenate([din_got, din_kept]))

    count = jnp.broadcast_to(jnp.sum(valid_counts.astype(F32)), (1, width))
    sums = jnp.concatenate([(kept + got)[8:], count, jnp.zeros((7, width), F32)])
    blocks, sums = sum_gradients(grad0, grad1, sums)
    d_in = jnp.concatenate([blocks[0], blocks[1], blocks[2]], axis=1).astype(F32)
    d_out = blocks[3].astype(F32)
    d_widen = jnp.concatenate([blocks[4], blocks[5], blocks[6], blocks[7]], axis=1).astype(F32)
    d_narrow = blocks[8:12].reshape(-1, width).astype(F32)
    squares, back, total = jnp.sum(sums[0:3], axis=1), sums[8:20], sums[24, 0]
    stream_rms = jnp.sqrt(squares / (total * width))
    return (
        section_cls[None],
        input_grads[None],
        d_in[None],
        back[0:2][None],
        d_out[None],
        back[2:3],
        back[3:5][None],
        back[5:7][None],
        d_widen[None],
        back[7:11].reshape(1, -1),
        d_narrow[None],
        back[11:12],
        stream_rms[None],
    )


def solution(mesh):
    placed = (
        P("dp", None),
        P("dp", None),
        P("dp", None),
        P("dp"),
        P("section", None, None),
        P("section", None, None),
        P("section", None, None),
        P("section", None),
        P("section", None, None),
        P("section", None, None),
        P("section", None, None),
        P("section", None),
        P("section", None, None),
        P("section", None),
        P("dp", None),
    )
    return jax.shard_map(
        local,
        mesh=mesh,
        in_specs=placed,
        out_specs=(
            P("section", "dp", None, None),
            P("section", "dp", None),
            P("section", None, None),
            P("section", None, None),
            P("section", None, None),
            P("section", None),
            P("section", None, None),
            P("section", None, None),
            P("section", None, None),
            P("section", None),
            P("section", None, None),
            P("section", None),
            P("section", None),
        ),
        check_vma=False,
    )
```

time: 1410 us -> 457 us (0.32)
  waiting for transfers between devices: 687 us -> 11.1 us
  Pallas kernels: 0 us -> 394 us
  matrix products: 392 us -> 0 us
  other arithmetic: 144 us -> 32.9 us
  blocking collectives: 77.1 us -> 0 us
  local copies, waits for them, and re-layouts: 70 us -> 14.3 us
  between operations: 17.3 us -> 1.44 us
    reduce_scatter x4 -> x0, waiting for transfers between devices: 534 us -> none  [the longest x1 175 us: local(): lax.psum_scatter(grads[6], 'dp', scatter_dimension=0, tiled=True)]
    pallas_call x0 -> x5, Pallas kernels: none -> 394 us  [the longest x1 238 us: sum_gradients(): pl.pallas_call(functools.partial(sum_kernel, plan), out_shape=[jax.ShapeD...]
    dot_general x58 -> x0, matrix products: 392 us -> none  [the longest x12 124 us: matmul(): return jnp.dot(left, right, preferred_element_type=jnp.float32)]
    all_gather x4 -> x0, waiting for transfers between devices: 153 us -> none  [the longest x1 77.3 us: local(): lax.all_gather(big_shards[2].astype(jnp.bfloat16), 'dp', axis=0, tiled=True)]
    psum x1 -> x0, blocking collectives: 77.1 us -> none  [local(): lax.psum((grads[1], grads[3], grads[4], grads[5], grads[7], grads[9]), 'dp')]
    reduce_sum x22 -> x2, other arithmetic: 44.1 us -> 2.11 us  [the longest x1 1.26 us: local(): count = jnp.broadcast_to(jnp.sum(valid_counts.astype(F32)), (1, width))]
    broadcast_in_dim x8 -> x0, other arithmetic: 25.6 us -> none  [the longest x1 7.37 us: local(): big_totals[2][None]]
    convert_element_type x6 -> x0, local copies, waits for them, and re-layouts: 19.9 us -> none  [to_half(): return array.astype(jnp.bfloat16)]
  transfers between devices with their start and end apart: 12 -> 7, of which waited for: 7 -> 2; matrix products, arithmetic and copies ran while one was open for 16% -> 9% of each run, Pallas kernels for 0% -> 52%
where the time goes in v1:
time: 457 us; the launch traced here: 456 us
  Pallas kernels  394 us (86%)
  other arithmetic  32.9 us (7%)
  local copies, waits for them, and re-layouts  14.3 us (3%)
  waiting for transfers between devices  11.1 us (2%)
    pallas_call x1, Pallas kernels, sum_gradients(): pl.pallas_call(functools.partial(sum_kernel, plan), out_shape=[jax.ShapeD...  238 us
    pallas_call x2, Pallas kernels, backward(): pl.pallas_call(backward_kernel, out_shape=[jax.ShapeDtypeStruct((12, widt...  89.1 us
    pallas_call x2, Pallas kernels, forward(): pl.pallas_call(forward_kernel, out_shape=[jax.ShapeDtypeStruct(s, d) for...  66.4 us
    ppermute x7, waiting for transfers between devices, swap_sections(): return lax.ppermute(array, 'section', [(0, 1), (1, 0)])  11.1 us
  transfers between devices with their start and end apart: 7, of which 2 were waited for; matrix products, arithmetic and copies ran while one was open for 9% of the time, Pallas kernels for 52%

profile of v1, /device:TPU:0, one launch (start us, length us, event | category | flops | bytes accessed | tf_op | source)
XLA Modules:
  0.0 455.6 jit_solution(9137480751332588654)
XLA Ops:
  2.3 1.4 reduce.3
  3.7 1.7 concatenate.84.vec_own
  5.9 1.2 dynamic_slice.6
  7.2 1.3 convert_reduce_fusion
  8.4 0.7 pad.13.clone
  9.2 0.6 pad_add_fusion.1
  9.8 1.2 pad_add_fusion
  11.6 0.7 collective-permute-done.2.wout_peer
  12.3 10.3 %collective-permute-done.1.win_peer = bf16[768,2304]{1,0:T(8,128)(2,1)} collective-permute-done((bf16[768,2304]{1,0:T(8,128)(2,1)}, bf16[768,2304]{1,0:T(8,128)(2,1)}, u32[]{:S(2)}, u32[]{:S(2)}) %collective-permute-start.1) | collective-permute-done | bytes 3538976 | tf_op jit(solution)/shard_map/ppermute | solution.py:519
  22.7 1.7 broadcast_in_dim.17.seg_cols
  24.4 33.3 %forward_layer.2 = (bf16[512,2304]{1,0:T(8,128)(2,1)}, bf16[12,512,512]{2,1,0:T(8,128)(2,1)}, f32[512,768]{1,0:T(8,128)}, bf16[512,768]{1,0:T(8,128)(2,1)}, f32[...) custom-call(s32[4]{0:T(128)} %get-tuple-element.94.flags, ...), custom_call_target="tpu_custom_call" | custom-call | flops 8999999488 | bytes 40000000 | tf_op jit(solution)/shard_map/forward_layer/pallas_call | solution.py:227
  57.7 33.1 %forward_layer.3 = (bf16[512,2304]{1,0:T(8,128)(2,1)}, bf16[12,512,512]{2,1,0:T(8,128)(2,1)}, f32[512,768]{1,0:T(8,128)}, bf16[512,768]{1,0:T(8,128)(2,1)}, f32[...) custom-call(s32[4]{0:T(128)} %get-tuple-element.95.flags, ...), custom_call_target="tpu_custom_call" | custom-call | flops 8999999488 | bytes 40000000 | tf_op jit(solution)/shard_map/forward_layer/pallas_call | solution.py:227
  90.8 0.8 constant_dynamic-update-slice_fusion.3
  91.7 44.6 %backward_layer.2 = (bf16[12,768,768]{2,1,0:T(8,128)(2,1)}, f32[512,768]{1,0:T(8,128)}, bf16[1,512,768]{2,1,0:T(8,128)(2,1)}, f32[16,768]{1,0:T(8,128)}) custom-call(s32[3]{0:T(128)} %get-tuple-element.97.flags, f32[24,768]{1,0:T(8,128)} %copy-done.2, f32[24,768]{1,0:T(8,128)} %copy-done.5, bf16[2,512,768]{2,1,0:T(8,128)(2,1)} %bitcast.79, ...), custom_call_target="tpu_custom_call" | custom-call | flops 17999998976 | bytes 60000000 | tf_op jit(solution)/shard_map/backward_layer/pallas_call | solution.py:471
  136.3 0.8 constant_dynamic-update-slice_fusion.2
  137.1 44.5 %backward_layer.3 = (bf16[12,768,768]{2,1,0:T(8,128)(2,1)}, f32[512,768]{1,0:T(8,128)}, bf16[1,512,768]{2,1,0:T(8,128)(2,1)}, f32[16,768]{1,0:T(8,128)}) custom-call(s32[3]{0:T(128)} %get-tuple-element.96.flags, f32[24,768]{1,0:T(8,128)} %copy-done.2, f32[24,768]{1,0:T(8,128)} %copy-done.5, bf16[1,512,768]{2,1,0:T(8,128)(2,1)} %get-tuple-element.57.g_any, ...), custom_call_target="tpu_custom_call" | custom-call | flops 17999998976 | bytes 60000000 | tf_op jit(solution)/shard_map/backward_layer/pallas_call | solution.py:471
  181.6 0.8 constant_dynamic-update-slice_fusion
  182.8 2.1 select_bitcast_fusion
  185.2 0.7 maximum_maximum_fusion.small_in
  185.9 238.0 %sum_gradients.1 = (bf16[9216,768]{1,0:T(8,128)(2,1)}, f32[32,768]{1,0:T(8,128)}) custom-call(bf16[9216,768]{1,0:T(8,128)(2,1)} %bitcast.59, bf16[9216,768]{1,0:T(8,128)(2,1)} %bitcast.58, f32[32,768]{1,0:T(8,128)} %maximum_maximum_fusion.small_in), custom_call_target="tpu_custom_call" | custom-call | flops 10000000 | bytes 60000000 | tf_op jit(solution)/shard_map/sum_gradients/pallas_call | solution.py:749
  423.9 1.2 slice.97
  425.1 0.9 slice_reduce_fusion
  426.0 0.8 slice_bitcast_fusion.9
  426.8 1.5 slice_bitcast_fusion.10
  428.2 1.3 fusion
  429.6 5.2 %slice_bitcast_fusion.3 = (bf16[1,768,768]{2,1,0:T(8,128)(2,1)S(1)}, bf16[1,768,768]{2,1,0:T(8,128)(2,1)S(1)}, bf16[1,768,768]{2,1,0:T(8,128)(2,1)S(1)}, bf16[1,...) fusion(bf16[9216,768]{1,0:T(8,128)(2,1)} %get-tuple-element.75), kind=kLoop, calls=%fused_computation.9 | loop fusion | flops 589824 | bytes 20054016 | tf_op jit(solution)/shard_map/concatenate | solution.py:823
  434.8 0.6 copy.28
  436.6 0.6 maximum_select_fusion.1
  437.2 3.2 maximum_convert_fusion.1
  440.4 4.3 maximum_convert_fusion
  444.7 6.8 %bitcast_convert_fusion = f32[1,3072,768]{2,1,0:T(8,128)} fusion(bf16[9216,768]{1,0:T(8,128)(2,1)} %get-tuple-element.75), kind=kLoop, calls=%fused_computation.1 | loop fusion | flops 2359296 | bytes 14155776 | tf_op jit(solution)/shard_map/convert_element_type | solution.py:824
  451.5 4.0 maximum_select_fusion
  (37 shorter events, 4.0 us)
Async XLA Ops:
  0.6 10.4 %copy-start = (s32[2,8]{1,0:T(2,128)S(1)}, s32[2,8]{1,0:T(2,128)}, u32[]{:S(2)}) copy-start(s32[2,8]{1,0:T(2,128)} %param.17) | copy-start | bytes 196
  0.7 22.0 %collective-permute-start.3 = (bf16[768,3072]{1,0:T(8,128)(2,1)}, bf16[768,3072]{1,0:T(8,128)(2,1)}, u32[]{:S(2)}, u32[]{:S(2)}) collective-permute-start(bf16[768,3072]{1,0:T(8,128)(2,1)} %bitcast.64), channel_id=1, source_target_pairs={{0,16},{16,0},{1,17},{17,1},{2,18},{18,2},{3,19},{19,3},{4,20},{20... | collective-permute-start | bytes 14155784 | tf_op jit(solution)/shard_map/ppermute | solution.py:519
  1.2 21.5 %collective-permute-start.4 = (bf16[3072,768]{1,0:T(8,128)(2,1)}, bf16[3072,768]{1,0:T(8,128)(2,1)}, u32[]{:S(2)}, u32[]{:S(2)}) collective-permute-start(bf16[3072,768]{1,0:T(8,128)(2,1)} %bitcast.69), channel_id=1, source_target_pairs={{0,16},{16,0},{1,17},{17,1},{2,18},{18,2},{3,19},{19,3},{4,20},{20... | collective-permute-start | bytes 14155784 | tf_op jit(solution)/shard_map/ppermute | solution.py:519
  1.3 21.4 %collective-permute-start.1 = (bf16[768,2304]{1,0:T(8,128)(2,1)}, bf16[768,2304]{1,0:T(8,128)(2,1)}, u32[]{:S(2)}, u32[]{:S(2)}) collective-permute-start(bf16[768,2304]{1,0:T(8,128)(2,1)} %bitcast.74), channel_id=1, source_target_pairs={{0,16},{16,0},{1,17},{17,1},{2,18},{18,2},{3,19},{19,3},{4,20},{20... | collective-permute-start | bytes 10616840 | tf_op jit(solution)/shard_map/ppermute | solution.py:519
  1.7 10.6 %collective-permute-start.2 = (bf16[768,768]{1,0:T(8,128)(2,1)}, bf16[768,768]{1,0:T(8,128)(2,1)S(1)}, u32[]{:S(2)}, u32[]{:S(2)}) collective-permute-start(bf16[768,768]{1,0:T(8,128)(2,1)} %bitcast.82), channel_id=1, source_target_pairs={{0,16},{16,0},{1,17},{17,1},{2,18},{18,2},{3,19},{19,3},{4,20},{20... | collective-permute-start | bytes 3538952 | tf_op jit(solution)/shard_map/ppermute | solution.py:519
  5.4 19.0 %copy-start.2 = (f32[24,768]{1,0:T(8,128)}, f32[24,768]{1,0:T(8,128)S(1)}, u32[]{:S(2)}) copy-start(f32[24,768]{1,0:T(8,128)S(1)} %concatenate.84.vec_own) | copy-start | bytes 221188
  5.4 6.2 %collective-permute-start = (f32[24,768]{1,0:T(8,128)S(1)}, f32[24,768]{1,0:T(8,128)S(1)}, u32[]{:S(2)}, u32[]{:S(2)}) collective-permute-start(f32[24,768]{1,0:T(8,128)S(1)} %concatenate.84.vec_own), channel_id=1, source_target_pairs={{0,16},{16,0},{1,17},{17,1},{2,18},{18,2},{3,19},{19,3},{4,20},{20... | collective-permute-start | bytes 221192 | tf_op jit(solution)/shard_map/ppermute | solution.py:519
  11.6 12.8 %copy-start.5 = (f32[24,768]{1,0:T(8,128)}, f32[24,768]{1,0:T(8,128)S(1)}, u32[]{:S(2)}) copy-start(f32[24,768]{1,0:T(8,128)S(1)} %collective-permute-done.vec_peer) | copy-start | bytes 221188
  12.3 12.0 %copy-start.4 = (bf16[768,768]{1,0:T(8,128)(2,1)}, bf16[768,768]{1,0:T(8,128)(2,1)S(1)}, u32[]{:S(2)}) copy-start(bf16[768,768]{1,0:T(8,128)(2,1)S(1)} %collective-permute-done.2.wout_peer) | copy-start | bytes 3538948
  57.7 33.9 %copy-start.3 = (f32[16,768]{1,0:T(8,128)S(1)}, f32[16,768]{1,0:T(8,128)}, u32[]{:S(2)}) copy-start(f32[16,768]{1,0:T(8,128)} %get-tuple-element.45) | copy-start | bytes 147460
  182.4 2.7 collective-permute-start.5
  184.9 266.6 %collective-permute-start.6 = (f32[512,768]{1,0:T(8,128)S(1)}, f32[512,768]{1,0:T(8,128)}, u32[]{:S(2)}, u32[]{:S(2)}) collective-permute-start(f32[512,768]{1,0:T(8,128)S(1)} %get-tuple-element.86), channel_id=1, source_target_pairs={{0,16},{16,0},{1,17},{17,1},{2,18},{18,2},{3,19},{19,3},{4,20},{20... | collective-permute-start | bytes 4718600 | tf_op jit(solution)/shard_map/ppermute | solution.py:519
  451.5 4.0 copy-start.1
